TPU v7x, 32 devices: a whole 2x2x4 slice. The times are simulated.
32 devices in a mesh: dp: 2 (over x), fsdp: 16 (over z, y, core).
Axes of the slice: x: 2, y: 2, z: 4, core: 2. Of those that a mesh axis runs over, the one named last changes fastest.
Arguments:
- token_ids: int32 [8192], P(('dp', 'fsdp')), may hold values from 0 to 31999
- seq_lengths: int32 [32, 8], P(('dp', 'fsdp')), may hold values from 0 to 256, as said below
- noise: bfloat16 [8192, 256], P(('dp', 'fsdp')), may hold values from -6 to 6
- noise_level: float32 [8192], P(('dp', 'fsdp')), may hold values from 0.2 to 2
- table: bfloat16 [32000, 256], P('fsdp'), may hold values from -6 to 6
- w_in: bfloat16 [256, 1024], P('fsdp'), may hold values from -0.375 to 0.375
- b_in: bfloat16 [1024], P('fsdp'), may hold values from -3 to 3
- gain_first: bfloat16 [1024], P('fsdp'), may hold values from 0.25 to 1.75
- shift_first: bfloat16 [1024], P('fsdp'), may hold values from -3 to 3
- w_qkv: bfloat16 [1024, 3072], P('fsdp'), may hold values from -0.1875 to 0.1875
- w_out: bfloat16 [1024, 1024], P('fsdp'), may hold values from -0.75 to 0.75
- b_out: bfloat16 [1024], P('fsdp'), may hold values from -3 to 3
- gain_second: bfloat16 [1024], P('fsdp'), may hold values from 0.25 to 1.75
- shift_second: bfloat16 [1024], P('fsdp'), may hold values from -3 to 3
- w_up: bfloat16 [1024, 4096], P('fsdp'), may hold values from -0.1875 to 0.1875
- b_up: bfloat16 [4096], P('fsdp'), may hold values from -3 to 3
- w_down: bfloat16 [4096, 1024], P('fsdp'), may hold values from -0.09375 to 0.09375
- b_down: bfloat16 [1024], P('fsdp'), may hold values from -3 to 3
- cotangent: bfloat16 [8192, 1024], P(('dp', 'fsdp')), may hold values from -6 to 6
Outputs:
- activations: bfloat16 [8192, 1024], P(('dp', 'fsdp'))
- noise_grad: float32 [8192, 256], P(('dp', 'fsdp'))
- table_grad: float32 [32000, 256], P('fsdp')
- w_in_grad: float32 [256, 1024], P('fsdp')
- b_in_grad: float32 [1024], P('fsdp')
- gain_first_grad: float32 [1024], P('fsdp')
- shift_first_grad: float32 [1024], P('fsdp')
- w_qkv_grad: float32 [1024, 3072], P('fsdp')
- w_out_grad: float32 [1024, 1024], P('fsdp')
- b_out_grad: float32 [1024], P('fsdp')
- gain_second_grad: float32 [1024], P('fsdp')
- shift_second_grad: float32 [1024], P('fsdp')
- w_up_grad: float32 [1024, 4096], P('fsdp')
- b_up_grad: float32 [4096], P('fsdp')
- w_down_grad: float32 [4096, 1024], P('fsdp')
- b_down_grad: float32 [1024], P('fsdp')
Inputs may be any that keep to these rules, and one draw needn't show every extreme that they name: `seq_lengths`: each length is a multiple of 8, a row's lengths sum to 64 or more and to 256 at most; in every draw some row holds one sequence of exactly 256 tokens; slots may be empty.
All inputs are finite; a program needn't handle non-finite values.
Results may differ from a plain program's by a relative error of at most 0.014.
Values may be sent and summed in bfloat16 or wider, within the bound.
A program may use at most 192 MiB of HBM per device.

v0:
```python
import jax
import jax.numpy as jnp
from jax import lax
from jax.experimental import pallas as pl
from jax.experimental.pallas import tpu as pltpu
from jax.sharding import PartitionSpec as P

HEADS = 16
VOCAB = 32000


norm_eps = 1e-05


def standardize(resid):
    centred = resid - jnp.mean(resid, axis=-1, keepdims=True)
    spread = jnp.mean(centred * centred, axis=-1, keepdims=True)
    return centred * lax.rsqrt(spread + norm_eps)


def row_normalize(tok_rows):
    return tok_rows * lax.rsqrt(jnp.mean(tok_rows * tok_rows, axis=1, keepdims=True) + norm_eps)


def exact_gelu(pre_act):
    return jax.nn.gelu(pre_act, approximate=False)


def split_heads(projected):
    tok_count = projected.shape[0]
    width = projected.shape[1] // 3
    head_size = width // HEADS
    key_heads = projected[:, width : 2 * width].reshape(tok_count, HEADS, head_size)
    value_heads = projected[:, 2 * width :].reshape(tok_count, HEADS, head_size)
    row_block = min(512, tok_count)
    query_blocks = projected[:, :width].reshape(tok_count // row_block, row_block, HEADS, head_size)
    return (query_blocks, key_heads, value_heads, row_block)


def block_scores(query_block, key_heads, seg_block, segment):
    raw_scores = (
        jnp.einsum("qhd,khd->hqk", query_block, key_heads, preferred_element_type=jnp.float32)
        * 0.125
    )
    same_seq = seg_block[:, None] == segment[None, :]
    return jnp.where(same_seq[None, :, :], raw_scores, -1000000000.0)


def attention_forward(projected, segment):
    query_blocks, key_heads, value_heads, row_block = split_heads(projected)
    seg_blocks = segment.reshape(-1, row_block)

    def block_step(items_in):
        query_block, seg_block = items_in
        scores = block_scores(query_block, key_heads, seg_block, segment)
        row_max = jnp.max(scores, axis=-1, keepdims=True)
        exp_scores = jnp.exp(scores - row_max)
        row_total = jnp.sum(exp_scores, axis=-1, keepdims=True)
        soft_probs = (exp_scores / row_total).astype(jnp.bfloat16)
        attended = jnp.einsum(
            "hqk,khd->qhd", soft_probs, value_heads, preferred_element_type=jnp.float32
        )
        return (attended, (row_max + jnp.log(row_total))[:, :, 0])

    attended, log_total = lax.map(block_step, (query_blocks, seg_blocks))
    return (attended.reshape(projected.shape[0], -1), log_total)


def attention_backward(projected, segment, log_total, grad_attended):
    query_blocks, key_heads, value_heads, row_block = split_heads(projected)
    seg_blocks = segment.reshape(-1, row_block)
    grad_blocks = grad_attended.reshape(query_blocks.shape)

    def block_step(totals, items_in):
        grad_keys, grad_values = totals
        query_block, seg_block, log_block, grad_block = items_in
        scores = block_scores(query_block, key_heads, seg_block, segment)
        soft_probs = jnp.exp(scores - log_block[:, :, None])
        grad_values = grad_values + jnp.einsum(
            "hqk,qhd->khd",
            soft_probs.astype(jnp.bfloat16),
            grad_block,
            preferred_element_type=jnp.float32,
        )
        grad_probs = jnp.einsum(
            "qhd,khd->hqk", grad_block, value_heads, preferred_element_type=jnp.float32
        )
        grad_scores = soft_probs * (
            grad_probs - jnp.sum(grad_probs * soft_probs, axis=-1, keepdims=True)
        )
        scaled_grad = (grad_scores * 0.125).astype(jnp.bfloat16)
        grad_query = jnp.einsum(
            "hqk,khd->qhd", scaled_grad, key_heads, preferred_element_type=jnp.float32
        )
        grad_keys = grad_keys + jnp.einsum(
            "hqk,qhd->khd", scaled_grad, query_block, preferred_element_type=jnp.float32
        )
        return ((grad_keys, grad_values), grad_query.astype(jnp.bfloat16))

    zero_heads = jnp.zeros(key_heads.shape, jnp.float32)
    (grad_keys, grad_values), grad_queries = lax.scan(
        block_step, (zero_heads, zero_heads), (query_blocks, seg_blocks, log_total, grad_blocks)
    )
    tok_count = projected.shape[0]
    return jnp.concatenate(
        [
            grad_queries.reshape(tok_count, -1),
            grad_keys.astype(jnp.bfloat16).reshape(tok_count, -1),
            grad_values.astype(jnp.bfloat16).reshape(tok_count, -1),
        ],
        axis=1,
    )


def shards(
    token_ids,
    seq_lengths,
    noise,
    noise_level,
    table,
    w_in,
    b_in,
    gain_first,
    shift_first,
    w_qkv,
    w_out,
    b_out,
    gain_second,
    shift_second,
    w_up,
    b_up,
    w_down,
    b_down,
    cotangent,
):
    tok_count = token_ids.shape[0]
    row_count = table.shape[0]
    group_ids = lax.all_gather(token_ids, "fsdp", axis=0, tiled=True)
    first_row = lax.axis_index("fsdp") * row_count
    owned = (group_ids[:, None] == first_row + jnp.arange(row_count)[None, :]).astype(jnp.bfloat16)
    owned_rows = jnp.dot(owned, table, preferred_element_type=jnp.float32).astype(jnp.bfloat16)
    tok_rows = lax.psum_scatter(owned_rows, "fsdp", scatter_dimension=0, tiled=True)
    tok_rows = tok_rows.astype(jnp.float32)
    vectors = (b_in, gain_first, shift_first, b_out, gain_second, shift_second, b_up, b_down)
    vec_all = lax.all_gather(jnp.concatenate(vectors), "fsdp", axis=0, tiled=False)
    vec_at = [0]
    for vector in vectors:
        vec_at.append(vec_at[-1] + vector.shape[0])
    (
        b_in_all,
        gain_first_all,
        shift_first_all,
        b_out_all,
        gain_second_all,
        shift_second_all,
        b_up_all,
        b_down_all,
    ) = [vec_all[:, lo:hi].reshape(-1) for lo, hi in zip(vec_at[:-1], vec_at[1:])]
    w_in_all = lax.all_gather(w_in, "fsdp", axis=0, tiled=True)
    w_qkv_all = lax.all_gather(w_qkv, "fsdp", axis=0, tiled=True)
    w_out_all = lax.all_gather(w_out, "fsdp", axis=0, tiled=True)
    w_up_all = lax.all_gather(w_up, "fsdp", axis=0, tiled=True)
    w_down_all = lax.all_gather(w_down, "fsdp", axis=0, tiled=True)
    seq_ends = jnp.cumsum(seq_lengths[0], dtype=jnp.int32)
    positions = jnp.arange(tok_count, dtype=jnp.int32)
    segment = jnp.sum((positions[:, None] >= seq_ends[None, :]).astype(jnp.int32), axis=1)
    live_rows = (segment < seq_lengths.shape[1]).astype(jnp.float32)[:, None]
    embedded = row_normalize(tok_rows)
    scale_in = lax.rsqrt(1.0 + noise_level * noise_level)[:, None]
    scaled = ((embedded + noise_level[:, None] * noise.astype(jnp.float32)) * scale_in).astype(
        jnp.bfloat16
    )
    resid_in = jnp.dot(scaled, w_in_all, preferred_element_type=jnp.float32) + b_in_all.astype(
        jnp.float32
    )
    std_first, first_pull = jax.vjp(standardize, resid_in)
    normed_a = (
        std_first * gain_first_all.astype(jnp.float32) + shift_first_all.astype(jnp.float32)
    ).astype(jnp.bfloat16)
    projected = jnp.dot(normed_a, w_qkv_all, preferred_element_type=jnp.float32).astype(
        jnp.bfloat16
    )
    attended, log_total = attention_forward(projected, segment)
    attended = attended.astype(jnp.bfloat16)
    resid_mid = (
        resid_in
        + jnp.dot(attended, w_out_all, preferred_element_type=jnp.float32)
        + b_out_all.astype(jnp.float32)
    )
    std_second, second_pull = jax.vjp(standardize, resid_mid)
    normed_b = (
        std_second * gain_second_all.astype(jnp.float32) + shift_second_all.astype(jnp.float32)
    ).astype(jnp.bfloat16)
    pre_act = jnp.dot(normed_b, w_up_all, preferred_element_type=jnp.float32) + b_up_all.astype(
        jnp.float32
    )
    activated, gelu_pull = jax.vjp(exact_gelu, pre_act)
    hidden = activated.astype(jnp.bfloat16)
    resid_out = (
        resid_mid
        + jnp.dot(hidden, w_down_all, preferred_element_type=jnp.float32)
        + b_down_all.astype(jnp.float32)
    )
    activations = (resid_out * live_rows).astype(jnp.bfloat16)
    grad_out = cotangent.astype(jnp.float32) * live_rows
    grad_down = grad_out.astype(jnp.bfloat16)
    b_down_term = jnp.sum(grad_down.astype(jnp.float32), axis=0)
    w_down_term = jnp.einsum("tf,td->fd", hidden, grad_down, preferred_element_type=jnp.float32)
    grad_hidden = jnp.einsum("td,fd->tf", grad_down, w_down_all, preferred_element_type=jnp.float32)
    grad_act = gelu_pull(grad_hidden)[0].astype(jnp.bfloat16)
    b_up_term = jnp.sum(grad_act.astype(jnp.float32), axis=0)
    w_up_term = jnp.einsum("td,tf->df", normed_b, grad_act, preferred_element_type=jnp.float32)
    grad_nb = jnp.einsum("tf,df->td", grad_act, w_up_all, preferred_element_type=jnp.float32)
    gain_second_term = jnp.sum(grad_nb * std_second, axis=0)
    shift_second_term = jnp.sum(grad_nb, axis=0)
    grad_mid = grad_out + second_pull(grad_nb * gain_second_all.astype(jnp.float32))[0]
    grad_att = grad_mid.astype(jnp.bfloat16)
    b_out_term = jnp.sum(grad_att.astype(jnp.float32), axis=0)
    w_out_term = jnp.einsum("tc,td->cd", attended, grad_att, preferred_element_type=jnp.float32)
    grad_attended = jnp.einsum(
        "td,cd->tc", grad_att, w_out_all, preferred_element_type=jnp.float32
    ).astype(jnp.bfloat16)
    grad_proj = attention_backward(projected, segment, log_total, grad_attended)
    w_qkv_term = jnp.einsum("td,te->de", normed_a, grad_proj, preferred_element_type=jnp.float32)
    grad_na = jnp.einsum("te,de->td", grad_proj, w_qkv_all, preferred_element_type=jnp.float32)
    gain_first_term = jnp.sum(grad_na * std_first, axis=0)
    shift_first_term = jnp.sum(grad_na, axis=0)
    grad_in = grad_mid + first_pull(grad_na * gain_first_all.astype(jnp.float32))[0]
    grad_pin = grad_in.astype(jnp.bfloat16)
    b_in_term = jnp.sum(grad_pin.astype(jnp.float32), axis=0)
    w_in_term = jnp.einsum("te,td->ed", scaled, grad_pin, preferred_element_type=jnp.float32)
    grad_scaled = jnp.einsum("td,ed->te", grad_pin, w_in_all, preferred_element_type=jnp.float32)
    noise_grad = grad_scaled * noise_level[:, None] * scale_in
    grad_embedded = grad_scaled * scale_in
    all_ids = lax.all_gather(token_ids, ("dp", "fsdp"), axis=0, tiled=True)
    all_grads = lax.all_gather(
        grad_embedded.astype(jnp.bfloat16), ("dp", "fsdp"), axis=0, tiled=True
    )
    owners = (first_row + jnp.arange(row_count)[:, None] == all_ids[None, :]).astype(jnp.bfloat16)
    row_grad = jnp.dot(owners, all_grads, preferred_element_type=jnp.float32)
    own_table = table.astype(jnp.float32)
    unused_rows, table_pull = jax.vjp(row_normalize, own_table)
    table_part = table_pull(row_grad)[0]

    def reduce_matrix(term):
        part = lax.psum_scatter(
            term.astype(jnp.bfloat16), "fsdp", scatter_dimension=0, tiled=True
        )
        return lax.psum(part, "dp").astype(jnp.float32)

    vec_terms = (
        b_in_term,
        gain_first_term,
        shift_first_term,
        b_out_term,
        gain_second_term,
        shift_second_term,
        b_up_term,
        b_down_term,
    )
    shard_count = lax.axis_size("fsdp")
    vec_term = jnp.concatenate([v.reshape(shard_count, -1) for v in vec_terms], axis=1)
    vec_part = lax.psum(vec_term, ("dp", "fsdp"))
    own_vec = lax.dynamic_index_in_dim(vec_part, lax.axis_index("fsdp"), 0, keepdims=False)
    vec_grads = [own_vec[lo:hi] for lo, hi in zip(vec_at[:-1], vec_at[1:])]
    return (
        activations,
        noise_grad,
        table_part,
        reduce_matrix(w_in_term),
        vec_grads[0],
        vec_grads[1],
        vec_grads[2],
        reduce_matrix(w_qkv_term),
        reduce_matrix(w_out_term),
        vec_grads[3],
        vec_grads[4],
        vec_grads[5],
        reduce_matrix(w_up_term),
        vec_grads[6],
        reduce_matrix(w_down_term),
        vec_grads[7],
    )


BF = jnp.bfloat16
F32 = jnp.float32
MESH_ID = pl.DeviceIdType.MESH
SEM_COUNT = 400
ROW_UNROLL = 8
HEAD_UNROLL = 4
EACH_UNROLL = 4
VMEM_LIMIT = 63 * 2**20
NT = (((1,), (1,)), ((), ()))
TN = (((0,), (0,)), ((), ()))
DIAG, ACROSS, TWIN = 0, 1, 2
FLIPS = ((1, 1), (1, 0), (0, 1))


def mm(a, b):
    return jnp.dot(a, b, preferred_element_type=F32)


def mm_nt(a, b):
    return lax.dot_general(a, b, NT, preferred_element_type=F32)


def mm_tn(a, b):
    return lax.dot_general(a, b, TN, preferred_element_type=F32)


def part(start, size):
    return pl.ds(pl.multiple_of(start, size), size)


def as_row(pair):
    return jnp.concatenate([pair[0:1, :], pair[1:2, :]], axis=1)


def as_col(pair):
    eye = lax.broadcasted_iota(jnp.int32, (128, 128), 0) == lax.broadcasted_iota(
        jnp.int32, (128, 128), 1
    )
    cols = [
        jnp.sum(jnp.where(eye, pair[k : k + 1, :], 0.0), axis=1, keepdims=True) for k in (0, 1)
    ]
    return jnp.concatenate(cols, axis=0)


def norm_parts(v):
    centred = v - jnp.mean(v, axis=-1, keepdims=True)
    rstd = lax.rsqrt(jnp.mean(centred * centred, axis=-1, keepdims=True) + norm_eps)
    return centred * rstd, rstd


def norm_back(u, n, rstd):
    return rstd * (
        u - jnp.mean(u, axis=-1, keepdims=True) - n * jnp.mean(u * n, axis=-1, keepdims=True)
    )


def layer_kernel(
    ids_hbm, lengths_hbm, level_hbm, b_in_hbm, gain_a_hbm, shift_a_hbm, b_out_hbm, gain_b_hbm, shift_b_hbm,
    b_dn_hbm, b_up_hbm, noise_hbm, table, w_in_hbm, w_qkv_hbm, w_out_hbm, w_up_hbm, w_down_hbm, cot_hbm,
    act_hbm, ngrad_hbm, tgrad_hbm, vout_hbm, f_in_hbm, f_qkv_hbm, f_out_hbm, f_up_hbm, f_dn_hbm,
    ids_v, lengths_v, level_v, b_in_v, gain_a_v, shift_a_v, b_out_v, gain_b_v, shift_b_v, b_dn_v, b_up_v,
    small, noise, w_in, w_qkv, w_out, w_up, w_down, cot,
    act, ngrad, tgrad, vout, f_in, f_qkv, f_out, f_up, f_dn,
    sm, smx, gsm, vec, vg, vq, vgy, vgz, vgf, bup, lives, idr,
    tp, tok, sc, win, wqkv, wout, wup, wdn, s_in, s_qkv, s_out, s_up,
    rin, rmid, gmid, t1, t2, t3, t4, na, proj, pr, att, asend, nb, gd, hid, ga,
    xs, xr, gatt, go, g_in, g_qkv, g_out, g_dn,
    y_in, y_qkv, y_out, y_up, y_dn, z_in, z_qkv, z_out, z_up, z_dn,
    ss, rr, ls,
):
    x = lax.axis_index("dp")
    f = lax.axis_index("fsdp")
    z, y, c = f // 4, lax.rem(f // 2, 2), lax.rem(f, 2)
    q = 2 * z + y
    g = 2 * x + c
    rows_here = table.shape[0]

    def dev(dx, dz, dy, dc):
        xx = lax.rem(x + dx, 2)
        zz = lax.rem(z + dz, 4)
        yy = lax.rem(y + dy, 2)
        cc = lax.rem(c + dc, 2)
        return (xx, zz * 4 + yy * 2 + cc)

    twin = dev(0, 0, 0, 1)
    across = dev(1, 0, 0, 0)
    pair_y = dev(0, 0, 1, 0)
    relay_to = (x, jnp.where(z == 2, 3, 0) * 4 + y * 2 + c)
    rel_dev = [dev(dx, 0, 0, dc) for dx, dc in FLIPS]
    rel_g = [2 * lax.rem(x + dx, 2) + lax.rem(c + dc, 2) for dx, dc in FLIPS]
    other_c = 1 - c

    def far(d):
        return lax.rem(z + 4 - d, 4)

    def to(d):
        return lax.rem(z + d, 4)

    sems = [0]
    pending = []
    inner = jnp.logical_or(z == 1, z == 2)
    outer = jnp.logical_not(inner)

    class Link:
        def __init__(self):
            self.at = sems[0]
            sems[0] += 1
            assert sems[0] <= SEM_COUNT

        def send(self, src, dst, device, arrives=None, only=None):
            self.only = only
            self.copy = pltpu.make_async_remote_copy(
                src_ref=src, dst_ref=dst, send_sem=ss.at[self.at],
                recv_sem=rr.at[self.at if arrives is None else arrives],
                device_id=device, device_id_type=MESH_ID,
            )
            if only is None:
                self.copy.start()
            else:
                pl.when(only)(self.copy.start)
            pending.append(self)
            return self

        def sent(self):
            pending.remove(self)
            if self.only is None:
                self.copy.wait_send()
            else:
                pl.when(self.only)(self.copy.wait_send)

        def got(self, ref):
            arrived(self.at, ref)

    def arrived(at, ref):
        pltpu.make_async_remote_copy(
            src_ref=ref, dst_ref=ref, send_sem=ss.at[0], recv_sem=rr.at[at],
            device_id=twin, device_id_type=MESH_ID,
        ).wait_recv()

    def each_rows(count, size, body, unroll=ROW_UNROLL):
        def step(i, carry):
            body(part(i * size, size))
            return carry

        lax.fori_loop(0, count // size, step, 0, unroll=unroll)

    def each(count, body, unroll=EACH_UNROLL):
        def step(i, carry):
            body(i)
            return carry

        lax.fori_loop(0, count, step, 0, unroll=unroll)

    local = [0]
    stores = []

    def moved(src, dst):
        copy = pltpu.make_async_copy(src, dst, ls.at[local[0]])
        local[0] += 1
        copy.start()
        return copy

    vectors = (b_in_v, gain_a_v, shift_a_v, b_out_v, gain_b_v, shift_b_v, b_dn_v)
    load_small = [
        moved(src, dst)
        for src, dst in (
            (ids_hbm, ids_v), (lengths_hbm, lengths_v), (level_hbm, level_v), (b_in_hbm, b_in_v),
            (gain_a_hbm, gain_a_v), (shift_a_hbm, shift_a_v), (b_out_hbm, b_out_v),
            (gain_b_hbm, gain_b_v), (shift_b_hbm, shift_b_v), (b_dn_hbm, b_dn_v), (b_up_hbm, b_up_v),
        )
    ]
    load_in = moved(w_in_hbm, w_in)
    load_qkv = moved(w_qkv_hbm, w_qkv)
    load_cot = moved(cot_hbm, cot)
    own_table = moved(table, tp.at[c, pl.ds(0, rows_here)])
    load_noise = moved(noise_hbm, noise)
    load_out = moved(w_out_hbm, w_out)
    load_up = moved(w_up_hbm, w_up)
    load_down = moved(w_down_hbm, w_down)

    barrier = pltpu.get_barrier_semaphore()
    peers = [dev(0, d, 0, dc) for d in (1, 2, 3) for dc in (0, 1)] + rel_dev + [pair_y]
    for peer in peers:
        pl.semaphore_signal(barrier, inc=1, device_id=peer, device_id_type=MESH_ID)
    pl.semaphore_wait(barrier, len(peers))

    class GroupGather:
        def __init__(self, at):
            self.at = at
            self.across = Link().send(at(g), at(g), across)
            self.twin = Link().send(at(g), at(g), twin)

        def hop(self):
            self.across.got(self.at(rel_g[ACROSS]))
            self.second = Link().send(self.at(rel_g[ACROSS]), self.at(rel_g[ACROSS]), twin)

        def got_twin(self):
            self.twin.got(self.at(rel_g[TWIN]))

        def got_diag(self):
            self.second.got(self.at(rel_g[DIAG]))

    class Gather:
        def __init__(self, whole, mine, theirs, height, twins=None, relay=True):
            self.whole, self.height, self.relay = whole, height, relay
            places = (self.sub(q, c), self.sub(q, c, twins))
            self.links = {}
            for d in (0, 2, 1, 3):
                only = {1: z != 3, 3: z != 0}.get(d) if relay else None
                for dc in (1, 0):
                    if (d, dc) != (0, 0):
                        self.links[d, dc] = Link().send(
                            theirs if dc else mine, places[dc], dev(0, d, 0, dc), only=only
                        )

        def sub(self, block, core, whole=None):
            whole = self.whole if whole is None else whole
            if self.height is None:
                return whole.at[block, core]
            return whole.at[block, part(core * self.height, self.height)]

        def over_y(self, block):
            return Link().send(self.whole.at[block], self.whole.at[block], pair_y)

        def own(self):
            self.links[0, 1].got(self.sub(q, other_c))
            self.y_own = self.over_y(q)

        def second(self):
            block = 2 * far(2) + y
            for dc in (1, 0):
                ref = self.sub(block, other_c if dc else c)
                self.links[2, dc].got(ref)
                if self.relay:
                    Link().send(
                        ref, ref, relay_to, only=inner,
                        arrives=jnp.where(z == 2, self.links[3, dc].at, self.links[1, dc].at),
                    )
            self.y_second = self.over_y(block)

        def near(self):
            self.y_near = self.one(3, 1)

        def last(self):
            self.y_last = self.one(1, 3)

        def one(self, low, high):
            block = 2 * jnp.where(z < 2, far(low), far(high)) + y
            for dc in (1, 0):
                arrived(
                    jnp.where(z < 2, self.links[low, dc].at, self.links[high, dc].at),
                    self.sub(block, other_c if dc else c),
                )
            return self.over_y(block)

        def forward(self):
            self.second()
            self.near()
            self.last()

        def finish(self):
            self.y_own.got(self.whole.at[2 * z + 1 - y])
            self.y_second.got(self.whole.at[2 * far(2) + 1 - y])
            self.y_near.got(self.whole.at[2 * jnp.where(z < 2, far(3), far(1)) + 1 - y])
            self.y_last.got(self.whole.at[2 * jnp.where(z < 2, far(1), far(3)) + 1 - y])

    class YFirstGather(Gather):
        def __init__(self, whole, mine, theirs, height):
            self.whole, self.height, self.relay = whole, height, True
            self.y_links = [
                Link().send(theirs if dc else mine, self.sub(q, c), dev(0, 0, 1, dc)) for dc in (0, 1)
            ]
            self.mine, self.theirs = mine, theirs

        def along(self):
            Gather.__init__(self, self.whole, self.mine, self.theirs, self.height)

        def cross(self):
            block = 2 * z + 1 - y
            for dc in (0, 1):
                self.y_links[dc].got(self.sub(block, other_c if dc else c))
            ref = self.whole.at[block]
            self.beside = {
                d: Link().send(ref, ref, dev(0, d, 0, 0), only={1: z != 3, 3: z != 0}.get(d))
                for d in (2, 1, 3)
            }

        def over_y(self, block):
            return None

        def second(self):
            Gather.second(self)
            ref = self.whole.at[2 * far(2) + 1 - y]
            self.beside[2].got(ref)
            Link().send(
                ref, ref, relay_to, only=inner,
                arrives=jnp.where(z == 2, self.beside[3].at, self.beside[1].at),
            )

        def finish(self):
            self.links[0, 1].got(self.sub(q, other_c))
            self.near()
            self.last()
            for d in (1, 3):
                self.beside[d].got(self.whole.at[2 * far(d) + 1 - y])

    for load in load_small:
        load.wait()
    lane_at = lax.broadcasted_iota(jnp.int32, (1, 128), 1)
    small[...] = jnp.zeros_like(small)

    def put_half(row, shard):
        small[row : row + 1, :] = jnp.where(
            lane_at // 64 == c, jnp.concatenate([shard, shard], axis=1), 0.0
        )

    def put_pair(row, line):
        small[row : row + 1, :] = line[:, 0:128]
        small[row + 1 : row + 2, :] = line[:, 128:256]

    for k, v in enumerate(vectors):
        put_half(k, v[...].astype(F32).reshape(1, 64))
    up_shard = b_up_v[...].astype(F32).reshape(1, 256)
    for k in range(4):
        put_half(7 + k, up_shard[:, 64 * k : 64 * k + 64])
    put_pair(16, ids_v[...].astype(F32).reshape(1, 256))
    put_pair(20, level_v[...].reshape(1, 256))
    lengths = lengths_v[...].astype(F32)
    slot_at = lax.broadcasted_iota(jnp.int32, lengths.shape, 1)
    spots = (
        lax.broadcasted_iota(jnp.int32, (2, 128), 0) * 128
        + lax.broadcasted_iota(jnp.int32, (2, 128), 1)
    ).astype(F32)
    slot_of = jnp.zeros((2, 128), F32)
    for k in range(8):
        end = jnp.sum(jnp.where(slot_at <= k, lengths, 0.0), axis=1, keepdims=True)
        slot_of += jnp.where(spots >= end, 1.0, 0.0)
    small[18:20, :] = slot_of
    sm[q, c] = small[...]
    small_links = [Link().send(small, gsm.at[rel], rel_dev[rel]) for rel in (DIAG, ACROSS)]
    gather_small = Gather(sm, small, small, None, relay=False)

    own_rows = tp.at[c, pl.ds(0, rows_here)]
    table_link = Link().send(table, own_rows, twin)
    spare = tp.shape[1] - rows_here
    if spare:
        for core in (0, 1):
            tp[core, pl.ds(rows_here, spare), :] = jnp.zeros((spare, tp.shape[2]), BF)

    def pack(whole, spare_buf, height, pick):
        mine, theirs = pick(g), pick(2 * x + other_c)
        whole[q, part(c * height, height), :] = mine
        spare_buf[...] = theirs

    h = w_qkv.shape[0]
    hin = w_in.shape[0]

    def cols(ref, start, size=256):
        return ref[:, part(start, size)]

    win_at, wout_at = win.at[g], wout.at[g]
    load_in.wait()
    load_qkv.wait()
    win_at[q, c] = cols(w_in, 256 * g)
    s_in[0] = cols(w_in, 256 * (2 * x + other_c))
    gather_in = Gather(win_at, win_at.at[q, c], s_in.at[0], None, win.at[2 * x + other_c], relay=False)
    pack(
        wqkv, s_qkv, h,
        lambda k: jnp.concatenate([cols(w_qkv, 1024 * n + 256 * k) for n in (0, 1, 2)], axis=1),
    )
    gather_qkv = Gather(wqkv, wqkv.at[q, part(c * h, h)], s_qkv, h)


    lives[:, 0:1] = jnp.where(as_col(small[18:20, :]) < 7.5, 1.0, 0.0)
    vg[...] = jnp.zeros_like(vg)

    def grad_down_rows(at):
        masked = cot[at, :].astype(F32) * lives[at, 0:1]
        gd[g, at, :] = masked.astype(BF)
        vg[6:7, :] += jnp.sum(masked, axis=0, keepdims=True)

    load_out.wait()
    pack(wout_at, s_out, h, lambda k: cols(w_out, 256 * k))
    gather_out = Gather(
        wout_at, wout_at.at[q, part(c * h, h)], s_out, h, wout.at[2 * x + other_c], relay=False
    )
    load_cot.wait()
    each_rows(256, 32, grad_down_rows)
    group_gd = GroupGather(lambda k: gd.at[k])

    gather_small.own()
    gather_small.forward()

    gather_in.own()
    gather_qkv.own()
    gather_small.finish()
    smx_link = Link().send(sm, smx, across)
    own_table.wait()
    table_link.got(tp.at[other_c, pl.ds(0, rows_here)])
    lane = lax.broadcasted_iota(jnp.int32, (256, tp.shape[1]), 1)

    def look_up(block):
        ids = as_col(sm[block, c, 16:18, :]).astype(jnp.int32)
        total = jnp.zeros((256, 256), F32)
        for core in (0, 1):
            first = (4 * z + 2 * y + core) * rows_here
            hit = jnp.where(lane == ids - first, 1.0, 0.0).astype(BF)
            total += mm(hit, tp[core])
        return total.astype(BF)

    emb_y = [Link() for _ in range(4)]
    for d in range(4):
        tok[d] = look_up(2 * to(d) + 1 - y)
        emb_y[d].send(tok.at[d], tok.at[8 + d], pair_y)

    load_down.wait()
    wdn[q, part(c * h, h), :] = w_down[part(g * h, h), :]
    gather_dn_y = YFirstGather(
        wdn.at[:, :, 512:1024], w_down.at[part(g * h, h), 512:1024],
        w_down.at[part((2 * x + other_c) * h, h), 512:1024], h,
    )

    def own_blocks(d):
        tok[4 + d] = look_up(2 * lax.rem(z + d, 4) + y)

    each(4, own_blocks, 1)
    emb_z = [None]
    for d in (1, 2, 3):
        emb_y[d].got(tok.at[8 + d])
        tok[4 + d] = tok[4 + d] + tok[8 + d]
        emb_z.append(Link().send(tok.at[4 + d], tok.at[11 + d], dev(0, d, 0, 0)))
    emb_y[0].got(tok.at[8])

    for load in (load_noise, load_up):
        load.wait()
    ct = lax.broadcasted_iota(jnp.int32, (h, 128), 1) < 64
    for j in range(8):
        first = w_up[:, part(128 * (4 * j + x), 128)].astype(F32)
        second = w_up[:, part(128 * (4 * j + 2 + x), 128)].astype(F32)
        low = jnp.where(ct, first, pltpu.roll(second, 64, 1)).astype(BF)
        high = jnp.where(ct, pltpu.roll(first, 64, 1), second).astype(BF)
        wup[q, part(c * h, h), 128 * j : 128 * j + 128] = jnp.where(c == 0, low, high)
        s_up[:, 128 * j : 128 * j + 128] = jnp.where(c == 0, high, low)
    gather_in.forward()
    gather_qkv.forward()
    for j in range(8):
        vec[:, 128 * j : 128 * j + 128] = sm[j, 0, 0:16, :] + sm[j, 1, 0:16, :]

    gather_out.own()
    gather_out.forward()
    gather_in.finish()
    group_in = GroupGather(lambda k: win.at[k])
    group_gd.hop()
    rows_sum = tok[4].astype(F32) + tok[8].astype(F32)
    for d in (1, 2, 3):
        emb_z[d].got(tok.at[11 + d])
        rows_sum += tok[11 + d].astype(F32)
    gather_up = Gather(wup, wup.at[q, part(c * h, h)], s_up, h)
    level = as_col(small[20:22, :])
    scale_in = lax.rsqrt(1.0 + level * level)
    embedded = rows_sum * lax.rsqrt(jnp.mean(rows_sum * rows_sum, axis=1, keepdims=True) + norm_eps)
    sc[g] = ((embedded + level * noise[...].astype(F32)) * scale_in).astype(BF)
    group_sc = GroupGather(lambda k: sc.at[k])

    group_in.hop()
    group_in.got_twin()
    group_in.got_diag()

    def win_mat(k):
        return win[k].reshape(256, 256)

    def first_norm(row, keep):
        for k in range(4):
            keep[:, 256 * k : 256 * k + 256] = (
                mm(sc[row], win_mat(k)) + vec[0:1, 256 * k : 256 * k + 256]
            )

        def chunk(at):
            n, _ = norm_parts(keep[at, :])
            na[row, at, :] = (n * vec[1:2, :] + vec[2:3, :]).astype(BF)

        each_rows(256, 32, chunk)

    def project(row):
        def block(k):
            at = part(k * 256, 256)
            proj[row, :, at] = mm(na[row], wqkv[:, :, at].reshape(1024, 256)).astype(BF)

        each(3, block)

    first_norm(g, rin)
    group_sc.hop()
    gather_up.own()
    group_sc.got_twin()
    first_norm(rel_g[TWIN], t1)
    first_norm(rel_g[ACROSS], t1)
    group_sc.got_diag()
    first_norm(rel_g[DIAG], t1)
    gather_qkv.finish()
    each(4, project, 1)
    gather_out.finish()
    group_out = GroupGather(lambda k: wout.at[k])

    head_of = lax.broadcasted_iota(jnp.int32, (1, 256), 1) // 64
    small_links[DIAG].got(gsm.at[DIAG])
    small_links[ACROSS].got(gsm.at[ACROSS])

    def attend(row, pair):
        same = as_col(pair) == as_row(pair)
        keys = proj[row, :, 256:512]
        values = proj[row, :, 512:768]
        queries = proj[row, :, 0:256]
        t2[...] = jnp.zeros_like(t2)

        def head(k):
            mine = head_of == k
            q_head = jnp.where(mine, queries, jnp.zeros_like(queries))
            scores = jnp.where(same, mm_nt(q_head, keys) * 0.125, -1e9)
            weights = jnp.exp(scores - jnp.max(scores, axis=-1, keepdims=True))
            low_probs = (weights / jnp.sum(weights, axis=-1, keepdims=True)).astype(BF)
            pr[row * 4 + k] = low_probs
            t2[...] += mm(low_probs, jnp.where(mine, values, jnp.zeros_like(values)))

        each(4, head, HEAD_UNROLL)
        return t2[...].astype(BF)

    att_links = []
    my_cols = part(256 * g, 256)
    for rel in range(3):
        pair = sm[q, other_c, 18:20, :] if rel == TWIN else gsm[rel, 18:20, :]
        asend[rel] = attend(rel_g[rel], pair)
        att_links.append(Link().send(asend.at[rel], att.at[:, my_cols], rel_dev[rel]))
        if rel == DIAG:
            gather_up.second()
            for d in range(4):
                emb_y[d].sent()
            for d in (1, 2, 3):
                emb_z[d].sent()
            gather_dn = Gather(
                wdn.at[:, :, 0:512], w_down.at[part(g * h, h), 0:512],
                w_down.at[part((2 * x + other_c) * h, h), 0:512], h,
            )
            gather_dn_y.along()
        if rel == ACROSS:
            gather_dn_y.cross()
    att[:, my_cols] = attend(g, small[18:20, :])
    gather_dn.own()
    group_out.hop()
    gather_up.near()
    gather_up.last()
    group_out.got_twin()
    group_out.got_diag()
    for rel in (TWIN, ACROSS, DIAG):
        att_links[rel].got(att.at[:, part(256 * rel_g[rel], 256)])

    def out_block(k):
        at = part(k * 256, 256)
        rmid[:, at] = rin[:, at] + mm(att[...], wout[k].reshape(1024, 256)) + vec[3:4, at]

    each(4, out_block)

    def second_norm(at):
        n, _ = norm_parts(rmid[at, :])
        nb[g, at, :] = (n * vec[4:5, :] + vec[5:6, :]).astype(BF)

    each_rows(256, 32, second_norm)
    nb_across = Link().send(nb.at[g], nb.at[g], across)
    nb_twin = Link().send(nb.at[g], nb.at[g], twin)
    nb_pass = Link()
    group_gd.got_twin()
    group_gd.got_diag()

    bup[...] = jnp.zeros_like(bup)
    for k in range(4):
        bup[0:1, :] += jnp.where(g == k, vec[7 + k : 8 + k, :], 0.0)

    def ff_hidden(row):
        def block(k):
            at = part(k * 256, 256)
            t2[...] = mm(nb[row], wup[:, :, at].reshape(1024, 256)) + bup[0:1, at]

            def chunk(rows_at):
                pre = t2[rows_at, :]
                cdf = 0.5 + 0.5 * lax.erf(pre * 0.7071067811865476)
                pdf = jnp.exp(-0.5 * pre * pre) * 0.3989422804014327
                t2[rows_at, :] = pre * cdf
                ga[row, rows_at, at] = (cdf + pre * pdf).astype(BF)

            each_rows(256, 32, chunk)
            hid[pl.ds(2 * row, 2), :, at] = t2[...].astype(BF).reshape(2, 128, 256)

        each(4, block)

    def ff_grad(row):
        def block(k):
            at = part(k * 256, 256)
            grad = mm_nt(gd[row], wdn[pl.ds(2 * k, 2)].reshape(256, 1024))
            ga_low = (grad * ga[row, :, at].astype(F32)).astype(BF)
            ga[row, :, at] = ga_low
            bup[1:2, at] += jnp.sum(ga_low.astype(F32), axis=0, keepdims=True)

        each(4, block)

    gather_dn.second()
    gather_up.finish()
    ff_hidden(g)
    gather_dn.near()
    gather_dn.last()
    gather_dn_y.second()
    nb_twin.got(nb.at[rel_g[TWIN]])
    ff_hidden(rel_g[TWIN])
    nb_across.got(nb.at[rel_g[ACROSS]])
    nb_pass.send(nb.at[rel_g[ACROSS]], nb.at[rel_g[ACROSS]], twin)
    ff_hidden(rel_g[ACROSS])
    nb_pass.got(nb.at[rel_g[DIAG]])
    ff_hidden(rel_g[DIAG])

    class GroupSum:
        def __init__(self, sends, gets, partial, puts=None, temp=None):
            self.sends, self.gets, self.partial = sends, gets, partial
            self.temp = t1 if temp is None else temp
            self.puts = gets if puts is None else puts

        def first(self):
            self.partial(rel_g[DIAG], self.sends[0])
            self.a = Link().send(self.sends[0], self.puts[0], twin)

        def second(self):
            self.partial(rel_g[ACROSS], self.temp)
            self.a.got(self.gets[0])

            def chunk(at):
                self.sends[1][at, :] = (
                    self.temp[at, :] + self.gets[0][at, :].astype(F32)
                ).astype(BF)

            each_rows(256, 32, chunk, 2)

        def second_send(self):
            self.b = Link().send(self.sends[1], self.puts[1], across)

        def third(self):
            self.partial(rel_g[TWIN], self.sends[2])
            self.c = Link().send(self.sends[2], self.puts[2], twin)

        def own(self, into):
            self.partial(g, into)
            self.into = into

        def total(self):
            self.c.got(self.gets[2])
            self.b.got(self.gets[1])

        def rows(self, at):
            return (
                self.into[at, :].astype(F32)
                + self.gets[1][at, :].astype(F32)
                + self.gets[2][at, :].astype(F32)
            )

        def release(self):
            for link in (self.a, self.b, self.c):
                link.sent()

    def slots(ref, places):
        return [ref.at[place] for place in places]

    def nb_partial(row, into):
        def block(k):
            into[:, part(k * 256, 256)] = mm_nt(
                ga[row], wup[pl.ds(2 * k, 2)].reshape(256, 1024)
            ).astype(into.dtype)

        each(4, block, 2)

    def out_partial(row, into):
        def block(k):
            at = part(k * 256, 256)
            into[:, at] = mm(
                hid[pl.ds(2 * row, 2)].reshape(256, 1024), wdn[:, :, at].reshape(1024, 256)
            ).astype(into.dtype)

        each(4, block, 2)

    class Scatter:
        def __init__(self, grad, y_buf, z_buf, final, height):
            self.grad, self.y_buf, self.z_buf, self.final, self.height = (
                grad, y_buf, z_buf, final, height,
            )

        def chunks(self, body):
            if self.height is None:
                each(2, body, 1)
            else:
                each_rows(2 * self.height, 32, body, 1)

        def half(self, core):
            if self.height is None:
                return self.grad.at[q, core]
            return self.grad.at[q, part(core * self.height, self.height)]

        def start(self, count=4):
            even = lax.rem(z, 2) == 0
            self.goals = (
                jnp.where(even, 3, 0), jnp.where(even, 1, 2), lax.rem(z + 2, 4), z,
            )
            self.y_links = []
            self.z_links = [Link() for _ in range(4)]
            self.more(count)

        def more(self, count=1):
            for _ in range(count):
                e = len(self.y_links)
                self.y_links.append(
                    Link().send(self.grad.at[2 * self.goals[e] + 1 - y], self.y_buf.at[e], pair_y)
                )

        def add_y(self, e):
            self.y_links[e].got(self.y_buf.at[e])
            block = 2 * self.goals[e] + y

            def chunk(at):
                self.grad[block, at] = (
                    self.grad[block, at].astype(F32) + self.y_buf[e, at].astype(F32)
                ).astype(BF)

            self.chunks(chunk)
            return self.grad.at[block]

        def end_to_end(self):
            ref = self.add_y(0)
            self.z_links[0].send(
                ref, self.z_buf.at[0], (x, (z + 1 - 2 * lax.rem(z, 2)) * 4 + y * 2 + c)
            )

        def near(self):
            ref = self.add_y(1)
            slot = jnp.where(inner, 2, 1)
            self.z_links[1].send(
                ref, self.z_buf.at[slot], (x, self.goals[1] * 4 + y * 2 + c),
                arrives=jnp.where(inner, self.z_links[2].at, self.z_links[1].at),
            )

        def second(self):
            ref = self.add_y(2)
            block = 2 * self.goals[2] + y

            def relayed():
                self.z_links[0].got(self.z_buf.at[0])

                def chunk(at):
                    self.grad[block, at] = (
                        self.grad[block, at].astype(F32) + self.z_buf[0, at].astype(F32)
                    ).astype(BF)

                self.chunks(chunk)

            pl.when(inner)(relayed)
            self.z_links[3].send(ref, self.z_buf.at[3], dev(0, 2, 0, 0))

        def own(self):
            self.add_y(3)

        def middle(self):
            self.end_to_end()
            self.near()
            self.second()
            self.own()

        def last(self):
            def summed(slots):
                def run():
                    for slot in slots:
                        self.z_links[slot].got(self.z_buf.at[slot])

                    def chunk(at):
                        total = self.grad[q, at].astype(F32)
                        for slot in slots:
                            total += self.z_buf[slot, at].astype(F32)
                        self.grad[q, at] = total.astype(BF)

                    self.chunks(chunk)

                return run

            pl.when(inner)(summed((1, 2, 3)))
            pl.when(outer)(summed((0, 3)))
            self.f_links = []
            for rel in range(3):
                core = lax.rem(c + FLIPS[rel][1], 2)
                self.f_links.append(
                    Link().send(
                        self.half(core),
                        self.final.at[g],
                        rel_dev[rel],
                    )
                )
            self.final[g] = self.half(c)[...]

        def finish(self):
            for rel in range(3):
                self.f_links[rel].got(self.final.at[rel_g[rel]])

    scatter_dn = Scatter(g_dn, y_dn, z_dn, f_dn, h)
    scatter_up = Scatter(hid, y_up, z_up, f_up, h)
    sum_out = GroupSum(slots(xs, (3, 4, 5)), slots(xr, (3, 4, 5)), out_partial)

    def dn_block(k):
        at = part(k * 256, 256)
        lhs = hid[:, :, at].reshape(1024, 256)
        g_dn[pl.ds(2 * k, 2)] = mm_tn(lhs, gd[...].reshape(1024, 1024)).astype(BF).reshape(
            2, 128, 1024
        )

    each(4, dn_block, 1)
    scatter_dn.start()
    gather_dn.finish()
    gather_dn_y.finish()
    sum_nb = GroupSum(slots(xs, (0, 1, 2)), slots(xr, (0, 1, 2)), nb_partial)
    ff_grad(rel_g[DIAG])
    sum_nb.first()
    ff_grad(rel_g[ACROSS])
    sum_nb.second()
    sum_nb.second_send()
    ff_grad(rel_g[TWIN])
    sum_nb.third()
    ff_grad(g)
    sum_out.first()
    sum_out.second()
    scatter_dn.end_to_end()
    sum_out.third()

    sum_out.own(act)

    def up_block(k):
        at = part(k * 256, 256)
        lhs = nb[:, :, at].reshape(1024, 256)
        hid[pl.ds(2 * k, 2)] = mm_tn(lhs, ga[...].reshape(1024, 1024)).astype(BF).reshape(
            2, 128, 1024
        )

    each(4, up_block, 1)
    scatter_up.start()

    scatter_dn.near()
    sum_nb.own(t1)
    sum_nb.total()

    def second_back(at):
        grad_nb = sum_nb.rows(at)
        n, rstd = norm_parts(rmid[at, :])
        vg[4:5, :] += jnp.sum(grad_nb * n, axis=0, keepdims=True)
        vg[5:6, :] += jnp.sum(grad_nb, axis=0, keepdims=True)
        mid = gd[g, at, :].astype(F32) + norm_back(grad_nb * vec[4:5, :], n, rstd)
        gmid[at, :] = mid
        low_mid = mid.astype(BF)
        gatt[1, at, :] = low_mid
        vg[3:4, :] += jnp.sum(low_mid.astype(F32), axis=0, keepdims=True)

    each_rows(256, 32, second_back)

    def grad_o_part(to_g):
        total = jnp.zeros((256, 256), F32)
        for k in range(4):
            total += mm_nt(
                gatt[1, :, 256 * k : 256 * k + 256], wout[k, pl.ds(2 * to_g, 2)].reshape(256, 256)
            )
        return total.astype(BF)

    for link in (nb_pass, nb_across, nb_twin, group_gd.second):
        link.sent()
    go_links = []
    for rel in range(3):
        att_links[rel].sent()
        asend[rel] = grad_o_part(rel_g[rel])
        go_links.append(Link().send(asend.at[rel], go.at[g], rel_dev[rel]))
    go[g] = grad_o_part(g)

    def wog_partial(k, into):
        for j in range(4):
            into[:, 256 * j : 256 * j + 256] = mm_tn(
                att[:, 256 * j : 256 * j + 256], gatt[1, :, part(256 * k, 256)]
            ).astype(into.dtype)

    sum_nb.release()
    scatter_dn.second()
    for rel in (TWIN, ACROSS, DIAG):
        go_links[rel].got(go.at[rel_g[rel]])
    sum_wog = GroupSum(
        slots(gd, rel_g), slots(nb, rel_g), wog_partial, slots(nb, (rel_g[ACROSS], g, g))
    )
    sum_wog.first()
    sum_wog.second()
    sum_wog.second_send()
    sum_wog.third()
    sum_wog.own(nb.at[g])

    def attend_back(row):
        keys = proj[row, :, 256:512]
        values = proj[row, :, 512:768]
        queries = proj[row, :, 0:256]
        grad_rows = go[row]
        zero = jnp.zeros_like(keys)
        for buf in (t2, t3, t4):
            buf[...] = jnp.zeros_like(buf)

        def head(k):
            mine = head_of == k
            probs = pr[row * 4 + k]
            g_head = jnp.where(mine, grad_rows, zero)
            t4[...] += mm_tn(probs, g_head)
            grad_p = mm_nt(g_head, values)
            wide = probs.astype(F32)
            grad_s = wide * (grad_p - jnp.sum(grad_p * wide, axis=-1, keepdims=True))
            low_s = (grad_s * 0.125).astype(BF)
            t2[...] += mm(low_s, jnp.where(mine, keys, zero))
            t3[...] += mm_tn(low_s, jnp.where(mine, queries, zero))

        each(4, head, HEAD_UNROLL)
        proj[row, :, 0:256] = t2[...].astype(BF)
        proj[row, :, 256:512] = t3[...].astype(BF)
        proj[row, :, 512:768] = t4[...].astype(BF)

    def na_partial(row, into):
        def block(k):
            into[:, part(k * 256, 256)] = mm_nt(
                proj[row], wqkv[pl.ds(2 * k, 2)].reshape(256, 768)
            ).astype(into.dtype)

        each(4, block)

    sum_na = GroupSum(slots(xs, (0, 1, 2)), slots(xr, (0, 1, 2)), na_partial)
    scatter_dn.own()
    attend_back(rel_g[DIAG])
    sum_na.first()
    scatter_up.end_to_end()
    attend_back(rel_g[ACROSS])
    sum_na.second()
    sum_na.second_send()
    attend_back(rel_g[TWIN])
    sum_na.third()
    scatter_up.near()
    sum_wog.total()
    scatter_out = Scatter(g_out, y_out, z_out, f_out, h)
    for j in range(4):
        at = slice(256 * j, 256 * j + 256)
        g_out[2 * j : 2 * j + 2] = (
            nb[g, :, at].astype(F32) + nb[rel_g[ACROSS], :, at].astype(F32)
            + nb[rel_g[TWIN], :, at].astype(F32)
        ).astype(BF).reshape(2, 128, 256)
    scatter_out.start()
    attend_back(g)
    sum_na.own(t1)

    scatter_qkv = Scatter(g_qkv, y_qkv, z_qkv, f_qkv, h)
    scatter_in = Scatter(g_in, y_in, z_in, f_in, None)

    def qkv_block(k):
        at = part(k * 256, 256)
        lhs = na[:, :, at].reshape(1024, 256)
        g_qkv[pl.ds(2 * k, 2)] = mm_tn(lhs, proj[...].reshape(1024, 768)).astype(BF).reshape(
            2, 128, 768
        )

    each(4, qkv_block)
    scatter_qkv.start()
    scatter_up.second()

    sum_na.total()

    def first_back(at):
        grad_na = sum_na.rows(at)
        n, rstd = norm_parts(rin[at, :])
        vg[1:2, :] += jnp.sum(grad_na * n, axis=0, keepdims=True)
        vg[2:3, :] += jnp.sum(grad_na, axis=0, keepdims=True)
        low_in = (gmid[at, :] + norm_back(grad_na * vec[1:2, :], n, rstd)).astype(BF)
        gatt[0, at, :] = low_in
        vg[0:1, :] += jnp.sum(low_in.astype(F32), axis=0, keepdims=True)

    each_rows(256, 32, first_back)
    for k in range(4):
        vg[7 + k : 8 + k, :] = jnp.where(g == k, bup[1:2, :], 0.0)
    for j in range(8):
        vq[j % 2, j // 2] = vg[:, 128 * j : 128 * j + 128]
    vy_link = Link().send(vq.at[1 - y], vgy, pair_y)

    grad_scaled = jnp.zeros((256, 256), F32)
    for k in range(4):
        grad_scaled += mm_nt(gatt[0, :, 256 * k : 256 * k + 256], win_mat(k))
    level = as_col(small[20:22, :])
    scale_in = lax.rsqrt(1.0 + level * level)
    ngrad[...] = grad_scaled * (level * scale_in)
    stores.append(moved(ngrad, ngrad_hbm))

    def set_at(other_x, other_y, other_core):
        return ((lax.rem(x + other_x, 2) * 2 + lax.rem(y + other_y, 2)) * 2 + lax.rem(c + other_core, 2)) * 4

    home = tok.at[set_at(0, 0, 0) + z]
    tok[set_at(0, 0, 0) + z] = (grad_scaled * scale_in).astype(BF)
    steps = {"own": z, "second": far(2), "near": jnp.where(z < 2, far(3), far(1)), "last": jnp.where(z < 2, far(1), far(3))}

    class Line:
        def __init__(self, ref, first):
            self.first = first
            self.links = {
                d: Link().send(ref, ref, dev(0, d, 0, 0), only={1: z != 3, 3: z != 0}.get(d))
                for d in (2, 1, 3)
            }

        def spot(self, step):
            return self.first + steps[step]

        def got(self, step):
            ref = tok.at[self.spot(step)]
            one, three = self.links[1].at, self.links[3].at
            if step == "second":
                self.links[2].got(ref)
                Link().send(ref, ref, relay_to, only=inner, arrives=jnp.where(z == 2, three, one))
            elif step == "near":
                arrived(jnp.where(z < 2, three, one), ref)
            else:
                arrived(jnp.where(z < 2, one, three), ref)
            return self.spot(step)

    line_own = Line(home, set_at(0, 0, 0))
    tok_x = {}
    by_y = ("own", "second")
    tok_y = {}
    tok_t = {}

    def to_twin(spot, own_plane, key):
        tok_t[own_plane, key] = Link().send(tok.at[spot], tok.at[spot], twin)

    tok_x[0, 0] = Link().send(home, home, across)
    tok_y["own"] = Link().send(home, home, pair_y)
    to_twin(set_at(0, 0, 0) + z, True, (0, "own"))
    sum_out.second_send()

    def wig_partial(k, into):
        into[...] = mm_tn(sc[g], gatt[0, :, part(256 * k, 256)]).astype(into.dtype)

    sum_wig = GroupSum(
        slots(pr, (0, 1, 2)), slots(go, rel_g), wig_partial, slots(go, (rel_g[ACROSS], g, g)), t2
    )
    sum_wig.first()
    scatter_out.end_to_end()
    sum_wig.second()
    sum_wig.second_send()
    sum_wig.third()
    sum_wig.own(t3)
    scatter_dn.last()

    beside = set_at(1, 0, 0) + z
    tok_x[0, 0].got(tok.at[beside])
    line_beside = Line(tok.at[beside], set_at(1, 0, 0))
    to_twin(beside, False, (0, "own"))
    tok_x[1, "own"] = Link().send(tok.at[beside], tok.at[beside], pair_y)

    def tok_from_z(step):
        spot = line_own.got(step)
        tok_y[step] = Link().send(tok.at[spot], tok.at[spot], pair_y)
        to_twin(spot, True, (0, step))

    def tok_from_y(step):
        spot = set_at(0, 1, 0) + steps[step]
        tok_y[step].got(tok.at[spot])
        if step not in by_y:
            tok_x[1, step] = Link().send(tok.at[spot], tok.at[spot], across)
        to_twin(spot, True, (1, step))

    def tok_beside(step):
        spot = line_beside.got(step)
        to_twin(spot, False, (0, step))
        if step in by_y:
            tok_x[1, step] = Link().send(tok.at[spot], tok.at[spot], pair_y)

    def tok_from_x(step):
        spot = set_at(1, 1, 0) + steps[step]
        tok_x[1, step].got(tok.at[spot])
        to_twin(spot, False, (1, step))

    smx_link.got(smx)
    for other_x in (0, 1):
        for yy in (0, 1):
            for core in (0, 1):
                source = sm if other_x == 0 else smx
                for zz in range(4):
                    idr[(other_x * 2 + yy) * 2 + core : (other_x * 2 + yy) * 2 + core + 1, 256 * zz : 256 * zz + 256] = (
                        as_row(source[2 * zz + yy, core, 16:18, :])
                    )

    tile = 400
    base = (f * rows_here).astype(F32)
    tile_row = lax.broadcasted_iota(jnp.int32, (tile, 1024), 0).astype(F32)

    def table_add(other_x, other_y, other_core, begin):
        spot = set_at(other_x, other_y, other_core)
        row = (other_x * 2 + lax.rem(y + other_y, 2)) * 2 + lax.rem(c + other_core, 2)
        ids = idr[pl.ds(row, 1), :] - base

        def block(k):
            at = part(k * tile, tile)
            hit = jnp.where(tile_row == ids - (k * tile).astype(F32), 1.0, 0.0).astype(BF)
            add = mm(hit, tok[pl.ds(spot, 4)].reshape(1024, 256))
            if begin:
                tgrad[at, :] = add
            else:
                tgrad[at, :] += add

        each(rows_here // tile, block, 1)

    def twin_set(from_x, other_y):
        for step in steps:
            tok_t[from_x == 0, (other_y, step)].got(tok.at[set_at(from_x, other_y, 1) + steps[step]])

    tok_from_z("second")
    tok_from_z("near")
    scatter_up.own()
    scatter_qkv.end_to_end()
    tok_from_z("last")
    tok_beside("second")
    table_add(0, 0, 0, True)
    scatter_up.last()
    scatter_out.near()
    tok_from_y("own")
    scatter_qkv.near()
    twin_set(0, 0)
    table_add(0, 0, 1, False)
    sum_wig.total()
    g_in[...] = (
        t3[...] + go[rel_g[ACROSS]].astype(F32) + go[rel_g[TWIN]].astype(F32)
    ).astype(BF).reshape(8, 2, 16, 256)
    scatter_in.start()
    vy_link.got(vgy)
    vq[y] = vq[y] + vgy[...]
    vz_links = [
        Link().send(vq.at[y, to(d)], vgz.at[d - 1], dev(0, d, 0, 0)) for d in (1, 2, 3)
    ]
    tok_from_y("second")
    scatter_qkv.second()
    tok_from_y("near")
    scatter_qkv.own()
    scatter_out.second()
    scatter_out.own()
    tok_from_y("last")
    table_add(0, 1, 0, False)
    tok_beside("near")
    tok_beside("last")
    table_add(1, 0, 0, False)
    twin_set(0, 1)
    table_add(0, 1, 1, False)
    scatter_in.middle()
    scatter_qkv.last()
    for d in (1, 2, 3):
        vz_links[d - 1].got(vgz.at[d - 1])
    vtot = vq[y, z] + vgz[0] + vgz[1] + vgz[2]
    vgf[3] = vtot
    vf_links = [Link().send(vgf.at[3], vgf.at[rel], rel_dev[rel]) for rel in range(3)]
    twin_set(1, 0)
    table_add(1, 0, 1, False)
    scatter_out.last()
    scatter_in.last()
    sum_out.total()

    def out_rows(at):
        whole = rmid[at, :] + sum_out.rows(at) + vec[6:7, :]
        act[at, :] = (whole * lives[at, 0:1]).astype(BF)

    each_rows(256, 32, out_rows)
    stores.append(moved(act, act_hbm))
    sum_out.release()

    for step in steps:
        tok_from_x(step)
    table_add(1, 1, 0, False)
    twin_set(1, 1)
    table_add(1, 1, 1, False)

    def table_rows(at):
        values = tp[c, at, :].astype(F32)
        r = lax.rsqrt(jnp.mean(values * values, axis=1, keepdims=True) + norm_eps)
        row_grad = tgrad[at, :]
        slope = jnp.mean(row_grad * values, axis=1, keepdims=True)
        tgrad[at, :] = r * row_grad - values * (r * r * r * slope)

    for k in range(rows_here // 200):
        at = pl.ds(k * 200, 200)
        table_rows(at)
        stores.append(moved(tgrad.at[at], tgrad_hbm.at[at]))

    for rel in range(3):
        vf_links[rel].got(vgf.at[rel])
    vout[...] = vgf[0] + vgf[1] + vgf[2] + vgf[3]
    for scatter in (scatter_dn, scatter_up, scatter_qkv, scatter_out, scatter_in):
        scatter.finish()
    for k, (src, dst) in enumerate(((f_in, f_in_hbm), (f_qkv, f_qkv_hbm), (f_out, f_out_hbm), (f_up, f_up_hbm), (f_dn, f_dn_hbm), (vout, vout_hbm))):
        stores.append(moved(src, dst))
    for link in list(pending):
        link.sent()
    for store in stores:
        store.wait()


def finish_kernel(
    act_in, ngrad_in, tgrad_in, vout, f_in_hbm, f_qkv_hbm, f_out_hbm, f_up_hbm, f_dn_hbm,
    act, ngrad, tgrad, w_in_hbm, b_in, gain_a, shift_a, w_qkv_hbm, w_out_hbm, b_out, gain_b, shift_b,
    w_up_hbm, b_up, w_dn_hbm, b_dn,
    act_v, ngrad_v, tgrad_v, f_in, f_qkv, f_out, f_up, f_dn, w_in, w_qkv, w_out, w_up, w_dn, sems,
):
    count = [0]

    def moved(src, dst):
        copy = pltpu.make_async_copy(src, dst, sems.at[count[0]])
        count[0] += 1
        copy.start()
        return copy

    load_up = moved(f_up_hbm, f_up)
    load_dn = moved(f_dn_hbm, f_dn)
    load_qkv = moved(f_qkv_hbm, f_qkv)
    load_out = moved(f_out_hbm, f_out)
    load_in = moved(f_in_hbm, f_in)
    passed = [(act_in, act_v, act), (ngrad_in, ngrad_v, ngrad)]
    tile = tgrad_v.shape[0] // 5
    for k in range(5):
        at = pl.ds(k * tile, tile)
        passed.append((tgrad_in.at[at], tgrad_v.at[at], tgrad.at[at]))
    passed = [(moved(src, via), via, dst) for src, via, dst in passed]
    stores = []
    c = lax.rem(lax.axis_index("fsdp"), 2)
    rows = jnp.where(c == 0, vout[...], pltpu.roll(vout[...], 64, 1))
    for k, ref in enumerate((b_in, gain_a, shift_a, b_out, gain_b, shift_b, b_dn)):
        ref[...] = rows[k, 0:64]
    for k in range(4):
        b_up[64 * k : 64 * k + 64] = rows[7 + k, 0:64]
    h = w_out.shape[0]
    low_half = lax.broadcasted_iota(jnp.int32, (h, 128), 1) < 64
    load_up.wait()
    for shard in range(16):
        at = slice(128 * (shard // 2), 128 * (shard // 2) + 128)
        for half in (0, 1):
            first, second = f_up[2 * half, :, at].astype(F32), f_up[2 * half + 1, :, at].astype(F32)
            if shard % 2 == 0:
                both = jnp.where(low_half, first, pltpu.roll(second, 64, 1))
            else:
                both = jnp.where(low_half, pltpu.roll(first, 64, 1), second)
            w_up[:, 256 * shard + 128 * half : 256 * shard + 128 * half + 128] = both
    stores.append(moved(w_up, w_up_hbm))
    for load, via, dst in passed:
        load.wait()
        stores.append(moved(via, dst))
    load_dn.wait()
    for g in range(4):
        w_dn[h * g : h * g + h, :] = f_dn[g].astype(F32)
    stores.append(moved(w_dn, w_dn_hbm))
    load_qkv.wait()
    for g in range(4):
        for n in range(3):
            w_qkv[:, 1024 * n + 256 * g : 1024 * n + 256 * g + 256] = f_qkv[
                g, :, 256 * n : 256 * n + 256
            ].astype(F32)
    stores.append(moved(w_qkv, w_qkv_hbm))
    load_out.wait()
    load_in.wait()
    for g in range(4):
        at = slice(256 * g, 256 * g + 256)
        w_in[:, at] = f_in[g].astype(F32)
        w_out[:, at] = f_out[g].astype(F32)
    stores.append(moved(w_out, w_out_hbm))
    stores.append(moved(w_in, w_in_hbm))
    for store in stores:
        store.wait()


def fused_shards(
    token_ids, seq_lengths, noise, noise_level, table, w_in, b_in, gain_first, shift_first, w_qkv,
    w_out, b_out, gain_second, shift_second, w_up, b_up, w_down, b_down, cotangent,
):
    raw = (
        token_ids, seq_lengths, noise_level, b_in, gain_first, shift_first, b_out, gain_second,
        shift_second, b_down, b_up,
    )
    vmem = pl.BlockSpec(memory_space=pltpu.VMEM)
    hbm = pl.BlockSpec(memory_space=pl.ANY)

    def shape(*dims, dtype=BF):
        return jax.ShapeDtypeStruct(dims, dtype)

    rows_here = table.shape[0]
    padded = -(-rows_here // 256) * 256
    outs = [
        shape(256, 1024), shape(256, 256, dtype=F32), shape(rows_here, 256, dtype=F32),
        shape(16, 128, dtype=F32), shape(4, 16, 256), shape(4, 64, 768), shape(4, 64, 256),
        shape(4, 64, 1024), shape(4, 64, 1024),
    ]

    held = [pltpu.VMEM(v.shape, v.dtype) for v in raw] + [pltpu.VMEM((24, 128), F32)]
    held += [pltpu.VMEM(v.shape, v.dtype) for v in (noise, w_in, w_qkv, w_out, w_up, w_down, cotangent)]
    held += [pltpu.VMEM(v.shape, v.dtype) for v in outs]

    def bf(*dims):
        return pltpu.VMEM(dims, BF)

    def fl(*dims):
        return pltpu.VMEM(dims, F32)

    scratch = [
        fl(8, 2, 24, 128), fl(8, 2, 24, 128), fl(2, 24, 128),
        fl(16, 1024), fl(16, 1024), fl(2, 4, 16, 128), fl(4, 16, 128), fl(3, 16, 128),
        fl(4, 16, 128), fl(8, 1024), fl(256, 128), fl(8, 1024),
        bf(2, padded, 256), bf(32, 256, 256), bf(4, 256, 256), bf(4, 8, 2, 16, 256),
        bf(8, 128, 768), bf(4, 8, 128, 256), bf(8, 128, 1024), bf(8, 128, 1024),
        bf(2, 16, 256), bf(64, 768), bf(64, 256), bf(64, 1024),
        fl(256, 1024), fl(256, 1024), fl(256, 1024), fl(256, 1024),
        fl(256, 256), fl(256, 256), fl(256, 256),
        bf(4, 256, 1024), bf(4, 256, 768), bf(16, 256, 256), bf(256, 1024), bf(3, 256, 256),
        bf(4, 256, 1024), bf(4, 256, 1024), bf(8, 128, 1024), bf(4, 256, 1024),
        bf(6, 256, 1024), bf(6, 256, 1024), bf(2, 256, 1024), bf(4, 256, 256),
        bf(8, 2, 16, 256), bf(8, 128, 768), bf(8, 128, 256), bf(8, 128, 1024),
        bf(4, 2, 16, 256), bf(4, 128, 768), bf(4, 128, 256), bf(4, 128, 1024), bf(4, 128, 1024),
        bf(4, 2, 16, 256), bf(4, 128, 768), bf(4, 128, 256), bf(4, 128, 1024), bf(4, 128, 1024),
        pltpu.SemaphoreType.DMA((SEM_COUNT,)), pltpu.SemaphoreType.DMA((SEM_COUNT,)),
        pltpu.SemaphoreType.DMA((45,)),
    ]
    parts = pl.pallas_call(
        layer_kernel,
        out_shape=outs,
        in_specs=[hbm] * 19,
        out_specs=[hbm] * len(outs),
        scratch_shapes=held + scratch,
        compiler_params=pltpu.CompilerParams(
            collective_id=0, has_side_effects=True, vmem_limit_bytes=VMEM_LIMIT
        ),
        cost_estimate=pl.CostEstimate(flops=40 * 10**9, bytes_accessed=30 * 10**6, transcendentals=0),
    )(*raw, noise, table, w_in, w_qkv, w_out, w_up, w_down, cotangent)
    f32 = lambda a: jax.ShapeDtypeStruct(a.shape, F32)
    finals = [
        outs[0], outs[1], outs[2], f32(w_in), f32(b_in), f32(gain_first), f32(shift_first),
        f32(w_qkv), f32(w_out), f32(b_out), f32(gain_second), f32(shift_second), f32(w_up),
        f32(b_up), f32(w_down), f32(b_down),
    ]
    return tuple(
        pl.pallas_call(
            finish_kernel,
            out_shape=finals,
            in_specs=[hbm] * 3 + [vmem] + [hbm] * 5,
            out_specs=[vmem if len(v.shape) == 1 else hbm for v in finals],
            scratch_shapes=[pltpu.VMEM(v.shape, v.dtype) for v in outs[:3] + outs[4:]]
            + [pltpu.VMEM(finals[k].shape, F32) for k in (3, 7, 8, 12, 14)]
            + [pltpu.SemaphoreType.DMA((24,))],
            compiler_params=pltpu.CompilerParams(vmem_limit_bytes=VMEM_LIMIT),
        )(*parts)
    )


def solution(mesh):
    in_specs = (
        P(("dp", "fsdp")),
        P(("dp", "fsdp"), None),
        P(("dp", "fsdp"), None),
        P(("dp", "fsdp")),
        P("fsdp", None),
        P("fsdp", None),
        P("fsdp"),
        P("fsdp"),
        P("fsdp"),
        P("fsdp", None),
        P("fsdp", None),
        P("fsdp"),
        P("fsdp"),
        P("fsdp"),
        P("fsdp", None),
        P("fsdp"),
        P("fsdp", None),
        P("fsdp"),
        P(("dp", "fsdp"), None),
    )
    out_specs = (
        P(("dp", "fsdp"), None),
        P(("dp", "fsdp"), None),
        P("fsdp", None),
        P("fsdp", None),
        P("fsdp"),
        P("fsdp"),
        P("fsdp"),
        P("fsdp", None),
        P("fsdp", None),
        P("fsdp"),
        P("fsdp"),
        P("fsdp"),
        P("fsdp", None),
        P("fsdp"),
        P("fsdp", None),
        P("fsdp"),
    )
    fused = mesh.shape["dp"] == 2 and mesh.shape["fsdp"] == 16
    body = fused_shards if fused else shards
    return jax.shard_map(body, mesh=mesh, in_specs=in_specs, out_specs=out_specs, check_vma=False)
```

profile of v0, /device:TPU:15, one launch (start us, length us, event | category | flops | bytes accessed | tf_op | source)
XLA Modules:
  0.0 209.9 jit_solution(10365281036002752586)
XLA Ops:
  0.7 203.7 %shard_map.306 = (bf16[256,1024]{1,0:T(8,128)(2,1)}, f32[256,256]{1,0:T(8,128)}, f32[2000,256]{1,0:T(8,128)}, f32[16,128]{1,0:T(8,128)}, bf16[4,16,256]{2,1,0:T(...) custom-call(s32[256]{0:T(256)} %ids_hbm.1, ...), custom_call_target="tpu_custom_call" | custom-call | flops 40000000000 | bytes 30000000 | tf_op jit(solution)/shard_map/pallas_call | solution.py:1610
  204.4 5.3 %shard_map.307 = (bf16[256,1024]{1,0:T(8,128)(2,1)}, f32[256,256]{1,0:T(8,128)}, f32[2000,256]{1,0:T(8,128)}, f32[16,1024]{1,0:T(8,128)}, f32[64]{0:T(128)}, /*i...) custom-call(bf16[256,1024]{1,0:T(8,128)(2,1)} %get-tuple-element.25., ...), custom_call_target="tpu_custom_call" | custom-call | tf_op jit(solution)/shard_map/pallas_call | solution.py:1628
where the time goes:
time: 214 us; the launch traced here: 210 us
  Pallas kernels  209 us (98%)
    pallas_call x1, Pallas kernels, fused_shards(): pl.pallas_call(layer_kernel, out_shape=outs, in_specs=[hbm] * 19, out_spe...  204 us
    pallas_call x1, Pallas kernels, fused_shards(): pl.pallas_call(finish_kernel, out_shape=finals, in_specs=[hbm] * 3 + [vme...  5.34 us

commit v1 on v0

--- a/solution.py
+++ b/solution.py
@@ -1162,10 +1162,11 @@
     go[g] = grad_o_part(g)
 
     def wog_partial(k, into):
-        for j in range(4):
-            into[:, 256 * j : 256 * j + 256] = mm_tn(
-                att[:, 256 * j : 256 * j + 256], gatt[1, :, part(256 * k, 256)]
-            ).astype(into.dtype)
+        def block(j):
+            at = part(256 * j, 256)
+            into[:, at] = mm_tn(att[:, at], gatt[1, :, part(256 * k, 256)]).astype(into.dtype)
+
+        each(4, block, 1)
 
     sum_nb.release()
     scatter_dn.second()

time: 214 us -> 214 us (level)
  no operation moved by 1% of the time
where the time goes in v1:
time: 214 us; the launch traced here: 210 us
  Pallas kernels  209 us (98%)
    pallas_call x1, Pallas kernels, fused_shards(): pl.pallas_call(layer_kernel, out_shape=outs, in_specs=[hbm] * 19, out_spe...  204 us
    pallas_call x1, Pallas kernels, fused_shards(): pl.pallas_call(finish_kernel, out_shape=finals, in_specs=[hbm] * 3 + [vme...  5.34 us

profile of v1, /device:TPU:15, one launch (start us, length us, event | category | flops | bytes accessed | tf_op | source)
XLA Modules:
  0.0 210.0 jit_solution(6709363715546950889)
XLA Ops:
  0.7 203.7 %shard_map.306 = (bf16[256,1024]{1,0:T(8,128)(2,1)}, f32[256,256]{1,0:T(8,128)}, f32[2000,256]{1,0:T(8,128)}, f32[16,128]{1,0:T(8,128)}, bf16[4,16,256]{2,1,0:T(...) custom-call(s32[256]{0:T(256)} %ids_hbm.1, ...), custom_call_target="tpu_custom_call" | custom-call | flops 40000000000 | bytes 30000000 | tf_op jit(solution)/shard_map/pallas_call | solution.py:1611
  204.3 5.3 %shard_map.307 = (bf16[256,1024]{1,0:T(8,128)(2,1)}, f32[256,256]{1,0:T(8,128)}, f32[2000,256]{1,0:T(8,128)}, f32[16,1024]{1,0:T(8,128)}, f32[64]{0:T(128)}, /*i...) custom-call(bf16[256,1024]{1,0:T(8,128)(2,1)} %get-tuple-element.25., ...), custom_call_target="tpu_custom_call" | custom-call | tf_op jit(solution)/shard_map/pallas_call | solution.py:1629
